TPU v7x, 256 devices: a whole 4x4x8 slice. The times are simulated.
256 devices in a mesh: tm: 8 (over y, core), space: 32 (over z, x).
Axes of the slice: x: 4, y: 4, z: 8, core: 2. Of those that a mesh axis runs over, the one named last changes fastest.
Arguments:
- footprint: bfloat16 [4096, 32, 4096], P(('tm', 'space')), may hold values from -0.375 to 0.375
- block_tile: int32 [4096, 1], P(('tm', 'space')), may hold values from 0 to 31; in each aligned block of 16 rows (0 to 15, 16 to 31, ...) at most 2 rows name the same one
- block_sub: int32 [4096], P(('tm', 'space')), may hold values from 0 to 15
- block_rows: int32 [4096], P(('tm', 'space')), may hold values from 1 to 32, 98304 in all
- obs_var: float32 [2, 131072], P(None, ('tm', 'space')), may hold values from 0.5 to 8
- prior_std: float32 [2, 256, 65536], P(None, 'tm', 'space'), may hold values from 0.2 to 1
- ar_rate: float32 [256, 65536], P('tm', 'space'), may hold values from 0.4 to 1
- iterate: float32 [2, 131072], P(None, ('tm', 'space')), may hold values from -6 to 6
- residual: float32 [2, 131072], P(None, ('tm', 'space')), may hold values from -20 to 20
- direction: float32 [2, 131072], P(None, ('tm', 'space')), may hold values from -20 to 20
Outputs:
- new_iterate: float32 [2, 131072], P(None, ('tm', 'space'))
- new_residual: float32 [2, 131072], P(None, ('tm', 'space'))
- new_direction: float32 [2, 131072], P(None, ('tm', 'space'))
Inputs may be any that keep to these rules, and one draw needn't show every extreme that they name: `block_tile`: among the blocks of one device at most 2 name the same space tile, and in every draw some device has 2 that do.
All inputs are finite; a program needn't handle non-finite values. No bound on the sum of `block_rows` on one device may be relied on, other than what follows from the above.
Results may differ from a plain program's by a relative error of at most 0.0026.
Values may be sent and summed in bfloat16 or wider, within the bound.
A program may use at most 64 MiB of HBM per device.

v0:
```python
import jax
import jax.numpy as jnp
from jax import lax
from jax.sharding import PartitionSpec as P


def from_behind(x, axis, by):
    length = lax.axis_size(axis)
    pairs = [(i, i + by) for i in range(length) if 0 <= i + by < length]
    return lax.ppermute(x, axis, pairs)


def combine(earlier, later):
    return (earlier[0] * later[0], later[0] * earlier[1] + later[1])


def per_device(
    footprint,
    block_tile,
    block_sub,
    block_rows,
    obs_var,
    prior_std,
    ar_rate,
    iterate,
    residual,
    direction,
):
    block_count, orows, flux_columns = footprint.shape
    right_count = iterate.shape[0]
    tsteps, scells = ar_rate.shape
    bcells = flux_columns // tsteps
    nsubs = scells // bcells
    tile_count = lax.axis_size("space")
    position_count = max(2, 2 * block_count // tile_count)
    row_index = jnp.arange(orows, dtype=jnp.int32)
    row_valid = (row_index[None, :] < block_rows[:, None]).astype(jnp.float32).reshape(-1)
    begin_iter = iterate * row_valid
    begin_res = residual * row_valid
    begin_dir = direction * row_valid
    destination = block_tile[:, 0]
    tile_matches = (
        destination[:, None] == jnp.arange(tile_count, dtype=jnp.int32)[None, :]
    ).astype(jnp.int32)
    preceding_count = jnp.cumsum(tile_matches, axis=0) - tile_matches
    position_index = destination * position_count + jnp.sum(preceding_count * tile_matches, axis=1)
    position_lookup = (
        jnp.arange(tile_count * position_count, dtype=jnp.int32)[:, None] == position_index[None, :]
    )
    desired_rows = jnp.sum(jnp.where(position_lookup, block_sub[None, :] + 1, 0), axis=1) - 1
    place_half = position_lookup.astype(jnp.bfloat16)
    dir_half = begin_dir.astype(jnp.bfloat16).reshape(right_count, block_count, orows)
    contrib = jnp.einsum(
        "bof,rbo->brf", footprint, dir_half, preferred_element_type=jnp.float32
    ).astype(jnp.bfloat16)
    departing_rows = jnp.dot(
        place_half,
        contrib.reshape(block_count, right_count * flux_columns),
        preferred_element_type=jnp.float32,
    ).astype(jnp.bfloat16)
    received_rows, arrived_sub = (
        lax.all_to_all(
            departing_rows.reshape(tile_count, position_count, right_count * flux_columns),
            "space",
            split_axis=0,
            concat_axis=0,
            tiled=True,
        ),
        lax.all_to_all(
            desired_rows.reshape(tile_count, position_count),
            "space",
            split_axis=0,
            concat_axis=0,
            tiled=True,
        ),
    )
    collect = (jnp.arange(nsubs, dtype=jnp.int32)[:, None] == arrived_sub.reshape(1, -1)).astype(
        jnp.bfloat16
    )
    summed = jnp.dot(
        collect,
        received_rows.reshape(tile_count * position_count, right_count * flux_columns),
        preferred_element_type=jnp.float32,
    )
    back = jnp.transpose(summed.reshape(nsubs, right_count, tsteps, bcells), (1, 2, 0, 3)).reshape(
        right_count, tsteps, scells
    )
    scaled = prior_std * back
    by_time = jnp.transpose(scaled, (1, 0, 2))
    rate_rows = ar_rate[:, None, :]
    fwd_rate, fwd_local = lax.associative_scan(combine, (rate_rows, by_time), axis=0)
    bwd_rate, bwd_local = lax.associative_scan(
        combine, (rate_rows, rate_rows * by_time), axis=0, reverse=True
    )
    from_below = jnp.zeros((right_count, scells), jnp.float32)
    from_above = jnp.zeros((right_count, scells), jnp.float32)
    for rounds in range(lax.axis_size("tm") - 1):
        from_below = from_behind(fwd_rate[-1] * from_below + fwd_local[-1], "tm", 1)
        from_above = from_behind(bwd_rate[0] * from_above + bwd_local[0], "tm", -1)
    forward = fwd_local + fwd_rate * from_below[None]
    backward = bwd_local + bwd_rate * from_above[None]
    ahead = jnp.concatenate([backward[1:], from_above[None]], axis=0)
    flux_half = (prior_std * jnp.transpose(forward + ahead, (1, 0, 2))).astype(jnp.bfloat16)
    gathered = lax.all_gather(flux_half, "space", axis=2, tiled=True)
    flux_table = jnp.transpose(
        gathered.reshape(right_count, tsteps, tile_count * nsubs, bcells), (2, 0, 1, 3)
    ).reshape(tile_count * nsubs, right_count * flux_columns)
    chooser = (
        jnp.arange(tile_count * nsubs, dtype=jnp.int32)[None, :]
        == (destination * nsubs + block_sub)[:, None]
    ).astype(jnp.bfloat16)
    block_flux = jnp.dot(chooser, flux_table, preferred_element_type=jnp.float32).astype(
        jnp.bfloat16
    )
    projected = jnp.einsum(
        "bof,brf->rbo",
        footprint,
        block_flux.reshape(block_count, right_count, flux_columns),
        preferred_element_type=jnp.float32,
    ).reshape(right_count, -1)
    image = projected * row_valid + obs_var * begin_dir
    res_norm, curvature = lax.psum(
        (jnp.sum(begin_res * begin_res, axis=1), jnp.sum(begin_dir * image, axis=1)),
        ("tm", "space"),
    )
    step_size = res_norm / curvature
    new_residual = begin_res - step_size[:, None] * image
    next_norm = lax.psum(jnp.sum(new_residual * new_residual, axis=1), ("tm", "space"))
    new_iterate = begin_iter + step_size[:, None] * begin_dir
    new_direction = new_residual + (next_norm / res_norm)[:, None] * begin_dir
    return (new_iterate, new_residual, new_direction)


def solution(mesh):
    return jax.shard_map(
        per_device,
        mesh=mesh,
        in_specs=(
            P(("tm", "space"), None, None),
            P(("tm", "space"), None),
            P(("tm", "space")),
            P(("tm", "space")),
            P(None, ("tm", "space")),
            P(None, "tm", "space"),
            P("tm", "space"),
            P(None, ("tm", "space")),
            P(None, ("tm", "space")),
            P(None, ("tm", "space")),
        ),
        out_specs=(P(None, ("tm", "space")), P(None, ("tm", "space")), P(None, ("tm", "space"))),
        check_vma=False,
    )
```

profile of v0, /device:TPU:1, one launch (start us, length us, event | category | flops | bytes accessed | tf_op | source)
XLA Modules:
  0.0 441.9 jit_solution(5835536150095913384)
XLA Ops:
  10.8 11.9 %all-to-all-start = ((s32[32,1,2]{2,1,0:T(1,128)}), s32[32,1,2]{2,1,0:T(1,128)S(1)}, u32[]{:S(2)}, u32[]{:S(2)}) async-start(s32[32,1,2]{2,1,0:T(1,128)} %bitcast.1), calls=%async_computation | async-start | bytes 32768 | tf_op jit(solution)/shard_map/all_to_all | solution.py:69
  28.7 5.8 %reverse.10 = f32[32,2048]{1,0:T(8,128)S(1)} reverse(f32[32,2048]{1,0:T(8,128)} %param.16), dimensions={0} | reverse | bytes 524288 | tf_op jit(solution)/shard_map/reverse.1
  38.3 2.8 convolution_convert_fusion.2
  44.0 9.2 %all-to-all-start.1 = ((bf16[32,2,8192]{2,1,0:T(2,128)(2,1)}), bf16[32,2,8192]{2,1,0:T(2,128)(2,1)S(1)}, u32[]{:S(2)}, u32[]{:S(2)}) async-start(bf16[32,2,8192]{2,1,0:T(2,128)(2,1)} %reshape.103), calls=%async_computation.1 | async-start | bytes 2097152 | tf_op jit(solution)/shard_map/all_to_all | solution.py:62
  56.4 7.9 %rev.12 = f32[32,1,2048]{2,0,1:T(8,128)} reverse(f32[32,1,2048]{2,0,1:T(8,128)} %add.332), dimensions={0} | reverse | bytes 524288 | tf_op jit(solution)/shard_map/rev | solution.py:92
  70.5 8.3 %all-to-all-done.1 = bf16[32,2,8192]{2,1,0:T(2,128)(2,1)S(1)} async-done(((bf16[32,2,8192]{2,1,0:T(2,128)(2,1)}), bf16[32,2,8192]{2,1,0:T(2,128)(2,1)S(1)}, u32[]{:S(2)}, u32[]{:S(2)}) %all-to-all-start.1) | async-done | bytes 1048608 | tf_op jit(solution)/shard_map/all_to_all | solution.py:62
  98.0 5.2 %collective-permute-start.7 = (f32[2,2048]{1,0:T(2,128)S(1)}, f32[2,2048]{1,0:T(2,128)S(1)}, u32[]{:S(2)}, u32[]{:S(2)}) collective-permute-start(f32[2,2048]{1,0:T(2,128)S(1)} %bitcast_add_fusion.6), channel_id=1, source_target_pairs={{32,0},{64,32},{96,64},{128,96},{160,128},{192,160},{224,192},{33,... | collective-permute-start | bytes 49160 | tf_op jit(solution)/shard_map/ppermute | solution.py:10
  111.9 3.1 collective-permute-start
  115.0 1.9 collective-permute-start.8
  117.0 3.6 collective-permute-start.1
  120.7 1.9 collective-permute-start.9
  122.6 3.6 collective-permute-start.2
  128.3 3.6 collective-permute-start.3
  133.9 3.6 collective-permute-start.4
  139.6 3.6 collective-permute-start.5
  145.2 3.8 collective-permute-start.6
  152.0 95.3 %all-gather.2.cloned.1.call-done = bf16[2,32,65536]{2,1,0:T(8,128)(2,1)} async-done(((bf16[2,32,2048]{2,1,0:T(8,128)(2,1)}), bf16[2,32,65536]{2,1,0:T(8,128)(2,1)}) %all-gather.2.cloned.1.call-update) | async-done | bytes 8388624 | tf_op jit(solution)/shard_map/all_gather | solution.py:104
  247.3 8.9 %copy.62 = bf16[8,8,512,128]{3,2,1,0:T(8,128)(2,1)} copy(bf16[8,8,512,128]{3,1,2,0:T(8,128)(2,1)} %bitcast.102) | data formatting | bytes 16777216
  256.2 7.6 %bitcast_bitcast_fusion = bf16[512,2,32,128]{3,0,2,1:T(8,128)(2,1)} fusion(bf16[2,32,512,128]{3,2,1,0:T(8,128)(2,1)} %bitcast.101), kind=kLoop, calls=%fused_computation.2 | loop fusion | bytes 16777216 | tf_op jit(solution)/shard_map/transpose | solution.py:105
  263.8 12.0 %copy.55 = bf16[512,2,32,128]{0,3,2,1:T(8,128)(2,1)} copy(bf16[512,2,32,128]{3,0,2,1:T(8,128)(2,1)} %bitcast_bitcast_fusion) | data formatting | bytes 16777216 | tf_op jit(solution)/shard_map/transpose | solution.py:105
  275.9 5.7 %convolution_convert_fusion.1 = bf16[16,8192]{1,0:T(8,128)(2,1)S(1)} fusion(bf16[512,8192]{0,1:T(8,128)(2,1)} %bitcast.100, s32[16]{0:T(128)S(1)} %copy-done.20), kind=kOutput, calls=%fused_computation.1 | convolution fusion | flops 134356992 | bytes 8650816 | tf_op jit(solution)/shard_map/dot_general | solution.py:112
  281.8 3.4 convolution_bitcast_fusion.1
  285.4 75.0 %all-reduce.40 = (f32[2]{0:T(128)S(1)}, f32[2]{0:T(128)S(1)}) all-reduce(f32[2]{0:T(128)S(1)} %get-tuple-element.4, f32[2]{0:T(128)S(1)} %get-tuple-element.3), channel_id=1, replica_groups=mesh['tm'=8,'space'=32] {'tm','space'}, use_global_device_ids=true, to_apply=%region_1.2 | all-reduce | flops 4 | bytes 32 | tf_op jit(solution)/shard_map/psum | solution.py:122
  361.3 73.1 %psum.23 = f32[2]{0:T(128)S(1)} all-reduce(f32[2]{0:T(128)S(1)} %get-tuple-element.7), channel_id=1, replica_groups=mesh['tm'=8,'space'=32] {'tm','space'}, use_global_device_ids=true, to_apply=%region_8.9 | all-reduce | flops 2 | bytes 16 | tf_op jit(solution)/shard_map/psum | solution.py:128
  (282 shorter events, 65.1 us)
Async XLA Ops:
  10.8 33.2 %all-to-all-start = ((s32[32,1,2]{2,1,0:T(1,128)}), s32[32,1,2]{2,1,0:T(1,128)S(1)}, u32[]{:S(2)}, u32[]{:S(2)}) async-start(s32[32,1,2]{2,1,0:T(1,128)} %bitcast.1), calls=%async_computation | async-start | bytes 32768 | tf_op jit(solution)/shard_map/all_to_all | solution.py:69
  27.2 14.0 %copy-start.2 = (f32[7,1,2048]{2,0,1:T(8,128)}, f32[7,1,2048]{2,0,1:T(8,128)S(1)}, u32[]{:S(2)}) copy-start(f32[7,1,2048]{2,0,1:T(8,128)S(1)} %slice.345) | copy-start | bytes 172036
  42.3 38.7 %copy-start = (f32[32,2048]{1,0:T(8,128)S(1)}, f32[32,2048]{1,0:T(8,128)}, u32[]{:S(2)}) copy-start(f32[32,2048]{1,0:T(8,128)} %param.16) | copy-start | bytes 786436
  42.3 38.7 %copy-start.1 = (f32[2,32,2048]{2,1,0:T(8,128)S(1)}, f32[2,32,2048]{2,1,0:T(8,128)}, u32[]{:S(2)}) copy-start(f32[2,32,2048]{2,1,0:T(8,128)} %param.15) | copy-start | bytes 1572868
  44.0 20.3 %copy-start.13 = (s32[32,1,2]{2,1,0:T(1,128)}, s32[32,1,2]{2,1,0:T(1,128)S(1)}, u32[]{:S(2)}) copy-start(s32[32,1,2]{2,1,0:T(1,128)S(1)} %all-to-all-done) | copy-start | bytes 772
  44.0 34.9 %all-to-all-start.1 = ((bf16[32,2,8192]{2,1,0:T(2,128)(2,1)}), bf16[32,2,8192]{2,1,0:T(2,128)(2,1)S(1)}, u32[]{:S(2)}, u32[]{:S(2)}) async-start(bf16[32,2,8192]{2,1,0:T(2,128)(2,1)} %reshape.103), calls=%async_computation.1 | async-start | bytes 2097152 | tf_op jit(solution)/shard_map/all_to_all | solution.py:62
  53.2 194.1 %all-gather.2.cloned.1.call-start = ((), (), s32[]{:S(2)}) async-start(), calls=%async_computation.2 | async-start | bytes 8650752 | tf_op jit(solution)/shard_map/all_gather | solution.py:104
  98.0 17.0 %collective-permute-start.7 = (f32[2,2048]{1,0:T(2,128)S(1)}, f32[2,2048]{1,0:T(2,128)S(1)}, u32[]{:S(2)}, u32[]{:S(2)}) collective-permute-start(f32[2,2048]{1,0:T(2,128)S(1)} %bitcast_add_fusion.6), channel_id=1, source_target_pairs={{32,0},{64,32},{96,64},{128,96},{160,128},{192,160},{224,192},{33,... | collective-permute-start | bytes 49160 | tf_op jit(solution)/shard_map/ppermute | solution.py:10
  111.9 5.1 %collective-permute-start = (f32[2,2048]{1,0:T(2,128)S(1)}, f32[2,2048]{1,0:T(2,128)S(1)}, u32[]{:S(2)}, u32[]{:S(2)}) collective-permute-start(f32[2,2048]{1,0:T(2,128)S(1)} %bitcast_add_fusion.13), channel_id=1, source_target_pairs={{0,32},{32,64},{64,96},{96,128},{128,160},{160,192},{192,224},{1,3... | collective-permute-start | bytes 49160 | tf_op jit(solution)/shard_map/ppermute | solution.py:10
  115.0 5.6 %collective-permute-start.8 = (f32[2,2048]{1,0:T(2,128)S(1)}, f32[2,2048]{1,0:T(2,128)S(1)}, u32[]{:S(2)}, u32[]{:S(2)}) collective-permute-start(f32[2,2048]{1,0:T(2,128)S(1)} %bitcast_add_fusion.5), channel_id=1, source_target_pairs={{32,0},{64,32},{96,64},{128,96},{160,128},{192,160},{224,192},{33,... | collective-permute-start | bytes 49160 | tf_op jit(solution)/shard_map/ppermute | solution.py:10
  117.0 5.6 %collective-permute-start.1 = (f32[2,2048]{1,0:T(2,128)S(1)}, f32[2,2048]{1,0:T(2,128)S(1)}, u32[]{:S(2)}, u32[]{:S(2)}) collective-permute-start(f32[2,2048]{1,0:T(2,128)S(1)} %bitcast_add_fusion.12), channel_id=1, source_target_pairs={{0,32},{32,64},{64,96},{96,128},{128,160},{160,192},{192,224},{1,3... | collective-permute-start | bytes 49160 | tf_op jit(solution)/shard_map/ppermute | solution.py:10
  120.7 5.6 %collective-permute-start.9 = (f32[2,2048]{1,0:T(2,128)S(1)}, f32[2,2048]{1,0:T(2,128)S(1)}, u32[]{:S(2)}, u32[]{:S(2)}) collective-permute-start(f32[2,2048]{1,0:T(2,128)S(1)} %bitcast_add_fusion.4), channel_id=1, source_target_pairs={{32,0},{64,32},{96,64},{128,96},{160,128},{192,160},{224,192},{33,... | collective-permute-start | bytes 49160 | tf_op jit(solution)/shard_map/ppermute | solution.py:10
  122.6 5.6 %collective-permute-start.2 = (f32[2,2048]{1,0:T(2,128)S(1)}, f32[2,2048]{1,0:T(2,128)S(1)}, u32[]{:S(2)}, u32[]{:S(2)}) collective-permute-start(f32[2,2048]{1,0:T(2,128)S(1)} %bitcast_add_fusion.11), channel_id=1, source_target_pairs={{0,32},{32,64},{64,96},{96,128},{128,160},{160,192},{192,224},{1,3... | collective-permute-start | bytes 49160 | tf_op jit(solution)/shard_map/ppermute | solution.py:10
  126.3 5.6 %collective-permute-start.10 = (f32[2,2048]{1,0:T(2,128)S(1)}, f32[2,2048]{1,0:T(2,128)S(1)}, u32[]{:S(2)}, u32[]{:S(2)}) collective-permute-start(f32[2,2048]{1,0:T(2,128)S(1)} %bitcast_add_fusion.3), channel_id=1, source_target_pairs={{32,0},{64,32},{96,64},{128,96},{160,128},{192,160},{224,192},{33,... | collective-permute-start | bytes 49160 | tf_op jit(solution)/shard_map/ppermute | solution.py:10
  128.3 5.6 %collective-permute-start.3 = (f32[2,2048]{1,0:T(2,128)S(1)}, f32[2,2048]{1,0:T(2,128)S(1)}, u32[]{:S(2)}, u32[]{:S(2)}) collective-permute-start(f32[2,2048]{1,0:T(2,128)S(1)} %bitcast_add_fusion.10), channel_id=1, source_target_pairs={{0,32},{32,64},{64,96},{96,128},{128,160},{160,192},{192,224},{1,3... | collective-permute-start | bytes 49160 | tf_op jit(solution)/shard_map/ppermute | solution.py:10
  132.0 5.6 %collective-permute-start.11 = (f32[2,2048]{1,0:T(2,128)S(1)}, f32[2,2048]{1,0:T(2,128)S(1)}, u32[]{:S(2)}, u32[]{:S(2)}) collective-permute-start(f32[2,2048]{1,0:T(2,128)S(1)} %bitcast_add_fusion.2), channel_id=1, source_target_pairs={{32,0},{64,32},{96,64},{128,96},{160,128},{192,160},{224,192},{33,... | collective-permute-start | bytes 49160 | tf_op jit(solution)/shard_map/ppermute | solution.py:10
  133.9 5.6 %collective-permute-start.4 = (f32[2,2048]{1,0:T(2,128)S(1)}, f32[2,2048]{1,0:T(2,128)S(1)}, u32[]{:S(2)}, u32[]{:S(2)}) collective-permute-start(f32[2,2048]{1,0:T(2,128)S(1)} %bitcast_add_fusion.9), channel_id=1, source_target_pairs={{0,32},{32,64},{64,96},{96,128},{128,160},{160,192},{192,224},{1,3... | collective-permute-start | bytes 49160 | tf_op jit(solution)/shard_map/ppermute | solution.py:10
  137.6 5.6 %collective-permute-start.12 = (f32[2,2048]{1,0:T(2,128)S(1)}, f32[2,2048]{1,0:T(2,128)S(1)}, u32[]{:S(2)}, u32[]{:S(2)}) collective-permute-start(f32[2,2048]{1,0:T(2,128)S(1)} %bitcast_add_fusion.1), channel_id=1, source_target_pairs={{32,0},{64,32},{96,64},{128,96},{160,128},{192,160},{224,192},{33,... | collective-permute-start | bytes 49160 | tf_op jit(solution)/shard_map/ppermute | solution.py:10
  139.6 5.6 %collective-permute-start.5 = (f32[2,2048]{1,0:T(2,128)S(1)}, f32[2,2048]{1,0:T(2,128)S(1)}, u32[]{:S(2)}, u32[]{:S(2)}) collective-permute-start(f32[2,2048]{1,0:T(2,128)S(1)} %bitcast_add_fusion.8), channel_id=1, source_target_pairs={{0,32},{32,64},{64,96},{96,128},{128,160},{160,192},{192,224},{1,3... | collective-permute-start | bytes 49160 | tf_op jit(solution)/shard_map/ppermute | solution.py:10
  143.3 5.8 %collective-permute-start.13 = (f32[2,2048]{1,0:T(2,128)S(1)}, f32[2,2048]{1,0:T(2,128)S(1)}, u32[]{:S(2)}, u32[]{:S(2)}) collective-permute-start(f32[2,2048]{1,0:T(2,128)S(1)} %bitcast_add_fusion), channel_id=1, source_target_pairs={{32,0},{64,32},{96,64},{128,96},{160,128},{192,160},{224,192},{33,... | collective-permute-start | bytes 49160 | tf_op jit(solution)/shard_map/ppermute | solution.py:10
  145.2 4.9 %collective-permute-start.6 = (f32[2,2048]{1,0:T(2,128)S(1)}, f32[2,2048]{1,0:T(2,128)S(1)}, u32[]{:S(2)}, u32[]{:S(2)}) collective-permute-start(f32[2,2048]{1,0:T(2,128)S(1)} %bitcast_add_fusion.7), channel_id=1, source_target_pairs={{0,32},{32,64},{64,96},{96,128},{128,160},{160,192},{192,224},{1,3... | collective-permute-start | bytes 49160 | tf_op jit(solution)/shard_map/ppermute | solution.py:10
  263.8 12.0 %copy-start.20 = (s32[16]{0:T(128)S(1)}, s32[16]{0:T(128)}, u32[]{:S(2)}) copy-start(s32[16]{0:T(128)} %get-tuple-element.34) | copy-start | bytes 196
  275.9 84.6 %copy-start.21 = (f32[2,512]{1,0:T(2,128)S(1)}, f32[2,512]{1,0:T(2,128)}, u32[]{:S(2)}) copy-start(f32[2,512]{1,0:T(2,128)} %param.17) | copy-start | bytes 12292
  361.3 73.8 %copy-start.19 = (f32[2,512]{1,0:T(2,128)}, f32[2,512]{1,0:T(2,128)S(1)}, u32[]{:S(2)}) copy-start(f32[2,512]{1,0:T(2,128)S(1)} %get-tuple-element.8) | copy-start | bytes 12292
  (15 other events, 107.6 us)
Sparse Core Ops, SparseCore 0:
  152.1 95.1 all-gather.1
where the time goes:
time: 446 us; the launch traced here: 442 us
  blocking collectives  148 us (33%)
  waiting for transfers between devices  104 us (23%)
  local copies, waits for them, and re-layouts  66.2 us (15%)
  starting transfers between devices  63 us (14%)
  other arithmetic  31.5 us (7%)
  between operations  15.6 us (3%)
  matrix products  13.8 us (3%)
    all_gather x1, waiting for transfers between devices, per_device(): gathered = lax.all_gather(flux_half, 'space', axis=2, tiled=True)  95.3 us
    psum x1, blocking collectives, per_device(): lax.psum((jnp.sum(begin_res * begin_res, axis=1), jnp.sum(begin_dir * ima...  75 us
    psum x1, blocking collectives, per_device(): lax.psum(jnp.sum(new_residual * new_residual, axis=1), ('tm', 'space'))  73.1 us
    ppermute x14, starting transfers between devices, from_behind(): return lax.ppermute(x, axis, pairs)  41.9 us
    transpose x2, local copies, waits for them, and re-layouts, per_device(): jnp.transpose(gathered.reshape(right_count, tsteps, tile_count * nsubs, b...  19.6 us
    all_to_all x1, starting transfers between devices, per_device(): lax.all_to_all(desired_rows.reshape(tile_count, position_count), 'space',...  11.9 us
    unnamed x49, local copies, waits for them, and re-layouts  10.2 us
    slice x28, local copies, waits for them, and re-layouts, per_device(): lax.associative_scan(combine, (rate_rows, by_time), axis=0)  9.76 us
  transfers between devices with their start and end apart: 17, of which 2 were waited for; matrix products, arithmetic and copies ran while one was open for 11% of the time, Pallas kernels for 0%

commit v1 on v0

v1 whole, which is shorter than its diff:
```python
import functools

import jax
import jax.numpy as jnp
from jax import lax
from jax.experimental import pallas as pl
from jax.experimental.pallas import tpu as pltpu
from jax.sharding import PartitionSpec as P

MESH = pl.DeviceIdType.MESH
F32 = jnp.float32
BF16 = jnp.bfloat16

NB, OB, TB, BC, SUB, CAP = 16, 32, 32, 128, 16, 2
ROWS, COLS = NB * OB, TB * BC
HALF = 16
CHUNKS = 4


def kernel(
    n_tm, n_sp, n_x,
    btile, bsub, brows, fp_hbm, prior_hbm, ar_hbm, obs, iterate, residual, direction,
    out_iter, out_res, out_dir,
    fp, prior, rate, cbuf, prod, dep1a, dep1b, rcv1a, rcv1b, dep2a, dep2b, rcv2a, rcv2b,
    meta_out, meta_in, meta_smem, first_of, second_of, onehot, back,
    coef, ends, ends_in_a, ends_in_b, rates_own, rates_in, local, carry, fluxa, fluxb, fbuf,
    red_own, red_tm, red_sum, red_sp,
    load_sem, send_sem, recv_sem, smem_sem,
):
    me = lax.axis_index("space")
    mt = lax.axis_index("tm")
    zpos, xpos = me // n_x, me % n_x
    n_z = n_sp // n_x

    def peer(k):
        return lax.rem(zpos + k // n_x, n_z) * n_x + lax.rem(xpos + k % n_x, n_x)

    def tpeer(k):
        return lax.rem(mt + k, n_tm)

    width = COLS // CHUNKS
    loads = []
    for c in range(CHUNKS):
        part = pl.ds(c * width, width)
        loads.append(pltpu.make_async_copy(fp_hbm.at[:, part], fp.at[:, part], load_sem.at[c]))
    load_rate = pltpu.make_async_copy(ar_hbm, rate, load_sem.at[CHUNKS])
    load_prior = pltpu.make_async_copy(prior_hbm, prior, load_sem.at[CHUNKS + 1])
    for copy in loads:
        copy.start()
    load_rate.start()
    load_prior.start()

    barrier = pltpu.get_barrier_semaphore()

    def greet_space(k, _):
        pl.semaphore_signal(barrier, inc=1, device_id={"space": peer(k)}, device_id_type=MESH)
        return 0

    def greet_tm(k, _):
        pl.semaphore_signal(barrier, inc=1, device_id={"tm": tpeer(k)}, device_id_type=MESH)
        return 0

    lax.fori_loop(1, n_sp, greet_space, 0)
    lax.fori_loop(1, n_tm, greet_tm, 0)

    lane = lax.broadcasted_iota(jnp.int32, (1, ROWS), 1)
    block_of = lane // OB
    limit = jnp.zeros((1, ROWS), jnp.int32)
    for b in range(NB):
        limit = jnp.where(block_of == b, brows[b], limit)
    valid = jnp.where(lane % OB < limit, 1.0, 0.0).astype(F32)
    begin_dir = direction[...] * valid
    begin_res = residual[...] * valid

    tiles = [btile[b, 0] for b in range(NB)]
    place = []
    for b in range(NB):
        count = jnp.int32(0)
        for e in range(b):
            count = count + jnp.where(tiles[e] == tiles[b], 1, 0)
        place.append(jnp.minimum(count, CAP - 1))

    row_j = lax.broadcasted_iota(jnp.int32, (n_sp, BC), 0)
    lane_j = lax.broadcasted_iota(jnp.int32, (n_sp, BC), 1)
    place_j = (lane_j // HALF) % CAP
    wanted = jnp.full((n_sp, BC), -1, jnp.int32)
    for b in range(NB):
        wanted = jnp.where((row_j == tiles[b]) & (place_j == place[b]), bsub[b], wanted)
    meta_out[...] = (wanted * HALF + lane_j % HALF).reshape(n_sp, 1, BC)

    rowb = lax.broadcasted_iota(jnp.int32, (NB, ROWS), 0)
    spread = jnp.concatenate(
        [jnp.where(rowb == block_of, begin_dir[r : r + 1, :], 0.0) for r in range(2)], axis=0
    ).astype(BF16)
    for c in range(CHUNKS):
        loads[c].wait()

        def product(i, _):
            col = pl.multiple_of(c * width + i * 2 * BC, 2 * BC)
            got = jnp.dot(spread, fp[:, pl.ds(col, 2 * BC)], preferred_element_type=F32)
            t = c * (width // BC) + 2 * i
            cbuf[pl.ds(t, 2 * NB, stride=TB), :] = got[:, :BC]
            cbuf[pl.ds(t + 1, 2 * NB, stride=TB), :] = got[:, BC:]
            return 0

        lax.fori_loop(0, width // (2 * BC), product, 0)

    for i in range(2 * NB):
        prod[i] = cbuf[i * TB : (i + 1) * TB, :].astype(BF16)

    pl.semaphore_wait(barrier, n_sp + n_tm - 2)

    def space_copy(src, dst, j, who, s):
        return pltpu.make_async_remote_copy(
            src_ref=src.at[j], dst_ref=dst.at[who], send_sem=send_sem.at[s], recv_sem=recv_sem.at[s],
            device_id={"space": j}, device_id_type=MESH,
        )

    def tm_copy(src, dst, k, s):
        return pltpu.make_async_remote_copy(
            src_ref=src, dst_ref=dst.at[mt], send_sem=send_sem.at[s], recv_sem=recv_sem.at[s],
            device_id={"tm": k}, device_id_type=MESH,
        )

    def all_arrived(buf, count, s):
        part = buf.at[pl.ds(0, count)]
        pltpu.make_async_copy(part, part, recv_sem.at[s]).wait()

    def all_left(buf, count, s):
        part = buf.at[pl.ds(0, count)]
        pltpu.make_async_copy(part, part, send_sem.at[s]).wait()

    def send_meta(k, _):
        space_copy(meta_out, meta_in, peer(k), me, 0).start()
        return 0

    lax.fori_loop(1, n_sp, send_meta, 0)
    meta_in[me] = meta_out[me]

    def fill_first(j):
        first, second = jnp.int32(0), jnp.int32(0)
        for b in range(NB - 1, -1, -1):
            hit = btile[b, 0] == j
            second = jnp.where(hit, first, second)
            first = jnp.where(hit, b, first)
        first_of[j] = first
        second_of[j] = second
        dep1a[j, 0] = prod[first]
        dep1a[j, 1] = prod[second]

    def fill_second(j):
        dep1b[j, 0] = prod[first_of[j] + NB]
        dep1b[j, 1] = prod[second_of[j] + NB]

    def send_first(k, _):
        j = peer(k)
        fill_first(j)
        space_copy(dep1a, rcv1a, j, me, 1).start()
        return 0

    def send_second(k, _):
        j = peer(k)
        fill_second(j)
        space_copy(dep1b, rcv1b, j, me, 2).start()
        return 0

    lax.fori_loop(1, n_sp, send_first, 0)
    fill_first(me)
    rcv1a[me] = dep1a[me]
    lax.fori_loop(1, n_sp, send_second, 0)
    fill_second(me)
    rcv1b[me] = dep1b[me]

    load_rate.wait()
    row8 = lax.broadcasted_iota(jnp.int32, (8, BC), 0)

    def last(v):
        return jnp.broadcast_to(v[7:8, :], (8, BC))

    def head(v):
        return jnp.broadcast_to(v[0:1, :], (8, BC))

    def coefficients(s, _):
        cols = pl.ds(pl.multiple_of(s * BC, BC), BC)
        fcum, bcum = [], []
        for v in range(4):
            a = rate[v * 8 : (v + 1) * 8, cols]
            rows = pl.ds(v * 8, 8)
            c1 = jnp.where(row8 >= 1, a, 0.0)
            p2 = a * jnp.where(row8 >= 1, pltpu.roll(a, 1, 0), 1.0)
            c2 = jnp.where(row8 >= 2, p2, 0.0)
            p4 = p2 * jnp.where(row8 >= 2, pltpu.roll(p2, 2, 0), 1.0)
            c4 = jnp.where(row8 >= 4, p4, 0.0)
            p8 = p4 * jnp.where(row8 >= 4, pltpu.roll(p4, 4, 0), 1.0)
            d1 = jnp.where(row8 <= 6, a, 0.0)
            q2 = a * jnp.where(row8 <= 6, pltpu.roll(a, 7, 0), 1.0)
            d2 = jnp.where(row8 <= 5, q2, 0.0)
            q4 = q2 * jnp.where(row8 <= 5, pltpu.roll(q2, 6, 0), 1.0)
            d4 = jnp.where(row8 <= 3, q4, 0.0)
            q8 = q4 * jnp.where(row8 <= 3, pltpu.roll(q4, 4, 0), 1.0)
            for i, value in enumerate((c1, c2, c4, p8, d1, d2, d4, q8)):
                coef[i, s, rows, :] = value
            fcum.append(p8)
            bcum.append(q8)
        for v in range(1, 4):
            fcum[v] = fcum[v] * last(fcum[v - 1])
        for v in range(2, -1, -1):
            bcum[v] = bcum[v] * head(bcum[v + 1])
        for v in range(4):
            coef[8, s, pl.ds(v * 8, 8), :] = fcum[v]
            above = head(bcum[v + 1]) if v < 3 else jnp.ones((8, BC), F32)
            coef[9, s, pl.ds(v * 8, 8), :] = jnp.where(row8 == 7, above, pltpu.roll(bcum[v], 7, 0))
        rates_own[pl.ds(s, 1), :] = fcum[3][7:8, :]
        return 0

    lax.fori_loop(0, SUB, coefficients, 0)

    def send_rates(k, _):
        tm_copy(rates_own, rates_in, tpeer(k), 3).start()
        return 0

    lax.fori_loop(1, n_tm, send_rates, 0)
    rates_in[mt] = rates_own[...]
    load_prior.wait()

    all_arrived(meta_in, n_sp - 1, 0)
    to_smem = pltpu.make_async_copy(meta_in, meta_smem, smem_sem.at[0])
    to_smem.start()
    quarter = lax.broadcasted_iota(jnp.int32, (1, BC), 1) // (CAP * HALF)
    target = lax.broadcasted_iota(jnp.int32, (SUB * HALF, BC), 0)
    for q in range(n_sp // 4):
        key = meta_in[4 * q]
        for g in range(1, 4):
            key = jnp.where(quarter == g, meta_in[4 * q + g], key)
        onehot[:, q * BC : (q + 1) * BC] = jnp.where(target == key, 1.0, 0.0).astype(BF16)
    to_smem.wait()
    all_arrived(rates_in, n_tm - 1, 3)

    def owner(r, rcv, flux, dep2, ends_in, s_in, s_ends, s_out):
        all_arrived(rcv, n_sp - 1, s_in)
        for h in range(2):
            part = rcv[:, :, h * HALF : (h + 1) * HALF, :].reshape(n_sp * CAP * HALF, BC)
            back[h] = jnp.dot(onehot[...], part, preferred_element_type=F32)

        def recursions(s, _):
            cols = pl.ds(pl.multiple_of(s * BC, BC), BC)
            fwd, bwd = [], []
            for v in range(4):
                rows = pl.ds(v * 8, 8)
                start = pl.multiple_of(s * HALF + (v % 2) * 8, 8)
                term = prior[r, v * 8 : (v + 1) * 8, cols] * back[v // 2, pl.ds(start, 8), :]
                y = term + coef[0, s, rows, :] * pltpu.roll(term, 1, 0)
                y = y + coef[1, s, rows, :] * pltpu.roll(y, 2, 0)
                y = y + coef[2, s, rows, :] * pltpu.roll(y, 4, 0)
                w = term * rate[v * 8 : (v + 1) * 8, cols]
                w = w + coef[4, s, rows, :] * pltpu.roll(w, 7, 0)
                w = w + coef[5, s, rows, :] * pltpu.roll(w, 6, 0)
                w = w + coef[6, s, rows, :] * pltpu.roll(w, 4, 0)
                fwd.append(y)
                bwd.append(w)
            for v in range(1, 4):
                fwd[v] = fwd[v] + coef[3, s, pl.ds(v * 8, 8), :] * last(fwd[v - 1])
            for v in range(2, -1, -1):
                bwd[v] = bwd[v] + coef[7, s, pl.ds(v * 8, 8), :] * head(bwd[v + 1])
            for v in range(4):
                above = head(bwd[v + 1]) if v < 3 else jnp.zeros((8, BC), F32)
                ahead = jnp.where(row8 == 7, above, pltpu.roll(bwd[v], 7, 0))
                local[s, pl.ds(v * 8, 8), :] = fwd[v] + ahead
            ends[r, 0, pl.ds(s, 1), :] = fwd[3][7:8, :]
            ends[r, 1, pl.ds(s, 1), :] = bwd[0][0:1, :]
            return 0

        lax.fori_loop(0, SUB, recursions, 0)

        def send_ends(k, _):
            who = tpeer(k)
            tm_copy(ends.at[r, jnp.where(who > mt, 0, 1)], ends_in, who, s_ends).start()
            return 0

        lax.fori_loop(1, n_tm, send_ends, 0)
        ends_in[mt] = jnp.zeros((SUB, BC), F32)
        all_arrived(ends_in, n_tm - 1, s_ends)
        below = jnp.zeros((SUB, BC), F32)
        for i in range(n_tm - 1):
            below = jnp.where(i < mt, rates_in[i] * below + ends_in[i], below)
        above = jnp.zeros((SUB, BC), F32)
        for i in range(n_tm - 1, 0, -1):
            above = jnp.where(i > mt, rates_in[i] * above + ends_in[i], above)
        carry[0] = below
        carry[1] = above

        def finish(s, _):
            cols = pl.ds(pl.multiple_of(s * BC, BC), BC)
            total = (
                local[s]
                + coef[8, s] * carry[0, pl.ds(s, 1), :]
                + coef[9, s] * carry[1, pl.ds(s, 1), :]
            )
            flux[s] = (prior[r, :, cols] * total).astype(BF16)
            return 0

        lax.fori_loop(0, SUB, finish, 0)

        def fill(j):
            for p in range(CAP):
                dep2[j, p] = flux[jnp.maximum(meta_smem[j, 0, p * HALF], 0) // HALF]

        def send_flux(k, _):
            j = peer(k)
            fill(j)
            space_copy(dep2, rcv2a if r == 0 else rcv2b, j, me, s_out).start()
            return 0

        lax.fori_loop(1, n_sp, send_flux, 0)
        fill(me)
        (rcv2a if r == 0 else rcv2b)[me] = dep2[me]

    owner(0, rcv1a, fluxa, dep2a, ends_in_a, 1, 4, 6)
    owner(1, rcv1b, fluxb, dep2b, ends_in_b, 2, 5, 7)

    images = []
    for r, (rcv, s_out) in enumerate(((rcv2a, 6), (rcv2b, 7))):
        all_arrived(rcv, n_sp - 1, s_out)
        for b in range(NB):
            fbuf[b * TB : (b + 1) * TB, :] = rcv[tiles[b], place[b]].astype(F32)

        def project(i, total):
            col = pl.multiple_of(i * 2 * BC, 2 * BC)
            left = jnp.concatenate(
                [fbuf[pl.ds(2 * i, NB, stride=TB), :], fbuf[pl.ds(2 * i + 1, NB, stride=TB), :]], axis=1
            ).astype(BF16)
            return total + lax.dot_general(
                left, fp[:, pl.ds(col, 2 * BC)], (((1,), (1,)), ((), ())), preferred_element_type=F32
            )

        total = lax.fori_loop(0, TB // 2, project, jnp.zeros((NB, ROWS), F32))
        images.append(jnp.sum(jnp.where(rowb == block_of, total, 0.0), axis=0, keepdims=True))
    image = jnp.concatenate(images, axis=0) * valid + obs[...] * begin_dir

    def partial(value):
        total = value[:, :BC]
        for i in range(1, ROWS // BC):
            total = total + value[:, i * BC : (i + 1) * BC]
        return total

    mine = jnp.concatenate(
        [
            partial(begin_res * begin_res),
            partial(begin_dir * image),
            partial(begin_res * image),
            partial(image * image),
        ],
        axis=0,
    )
    red_own[...] = mine
    red_tm[mt] = mine

    def send_tm_sum(k, _):
        tm_copy(red_own, red_tm, tpeer(k), 8).start()
        return 0

    lax.fori_loop(1, n_tm, send_tm_sum, 0)
    all_arrived(red_tm, n_tm - 1, 8)
    part = red_tm[0]
    for i in range(1, n_tm):
        part = part + red_tm[i]
    red_sum[...] = part
    red_sp[me] = part

    def send_sp_sum(k, _):
        j = peer(k)
        pltpu.make_async_remote_copy(
            src_ref=red_sum, dst_ref=red_sp.at[me], send_sem=send_sem.at[9], recv_sem=recv_sem.at[9],
            device_id={"space": j}, device_id_type=MESH,
        ).start()
        return 0

    lax.fori_loop(1, n_sp, send_sp_sum, 0)
    all_arrived(red_sp, n_sp - 1, 9)
    whole = jnp.sum(jnp.sum(red_sp[...], axis=0), axis=1, keepdims=True)
    res_norm, curvature, cross, square = (whole[2 * i : 2 * i + 2, :] for i in range(4))
    step = res_norm / curvature
    next_norm = res_norm - 2.0 * step * cross + step * step * square
    new_res = begin_res - step * image
    out_iter[...] = iterate[...] * valid + step * begin_dir
    out_res[...] = new_res
    out_dir[...] = new_res + (next_norm / res_norm) * begin_dir

    all_left(meta_out, n_sp - 1, 0)
    all_left(dep1a, n_sp - 1, 1)
    all_left(dep1b, n_sp - 1, 2)
    all_left(rates_in, n_tm - 1, 3)
    all_left(ends_in_a, n_tm - 1, 4)
    all_left(ends_in_b, n_tm - 1, 5)
    all_left(dep2a, n_sp - 1, 6)
    all_left(dep2b, n_sp - 1, 7)
    all_left(red_tm, n_tm - 1, 8)
    all_left(red_sp, n_sp - 1, 9)


def solution(mesh):
    n_tm, n_sp = mesh.shape["tm"], mesh.shape["space"]
    n_x = 4

    def per_device(footprint, block_tile, block_sub, block_rows, obs_var, prior_std, ar_rate, iterate, residual, direction):
        vmem = pl.BlockSpec(memory_space=pltpu.VMEM)
        smem = pl.BlockSpec(memory_space=pltpu.SMEM)
        hbm = pl.BlockSpec(memory_space=pl.ANY)
        slots = pltpu.VMEM((n_sp, CAP, TB, BC), BF16)
        state = pltpu.VMEM((n_tm, SUB, BC), F32)
        vector = jax.ShapeDtypeStruct(iterate.shape, F32)
        return pl.pallas_call(
            functools.partial(kernel, n_tm, n_sp, n_x),
            out_shape=(vector, vector, vector),
            in_specs=[smem, smem, smem, hbm, hbm, hbm, vmem, vmem, vmem, vmem],
            out_specs=(vmem, vmem, vmem),
            scratch_shapes=[
                pltpu.VMEM((ROWS, COLS), BF16),
                pltpu.VMEM(prior_std.shape, F32),
                pltpu.VMEM(ar_rate.shape, F32),
                pltpu.VMEM((2 * NB * TB, BC), F32),
                pltpu.VMEM((2 * NB, TB, BC), BF16),
                slots, slots, slots, slots, slots, slots, slots, slots,
                pltpu.VMEM((n_sp, 1, BC), jnp.int32),
                pltpu.VMEM((n_sp, 1, BC), jnp.int32),
                pltpu.SMEM((n_sp, 1, BC), jnp.int32),
                pltpu.SMEM((n_sp,), jnp.int32),
                pltpu.SMEM((n_sp,), jnp.int32),
                pltpu.VMEM((SUB * HALF, n_sp * CAP * HALF), BF16),
                pltpu.VMEM((2, SUB * HALF, BC), F32),
                pltpu.VMEM((10, SUB, TB, BC), F32),
                pltpu.VMEM((2, 2, SUB, BC), F32),
                state, state,
                pltpu.VMEM((SUB, BC), F32),
                state,
                pltpu.VMEM((SUB, TB, BC), F32),
                pltpu.VMEM((2, SUB, BC), F32),
                pltpu.VMEM((SUB, TB, BC), BF16),
                pltpu.VMEM((SUB, TB, BC), BF16),
                pltpu.VMEM((NB * TB, BC), F32),
                pltpu.VMEM((8, BC), F32),
                pltpu.VMEM((n_tm, 8, BC), F32),
                pltpu.VMEM((8, BC), F32),
                pltpu.VMEM((n_sp, 8, BC), F32),
                pltpu.SemaphoreType.DMA((CHUNKS + 2,)),
                pltpu.SemaphoreType.DMA((10,)),
                pltpu.SemaphoreType.DMA((10,)),
                pltpu.SemaphoreType.DMA((1,)),
            ],
            compiler_params=pltpu.CompilerParams(
                collective_id=0, has_side_effects=True, vmem_limit_bytes=40 << 20
            ),
            name="cg_step",
        )(
            block_tile, block_sub, block_rows, footprint.reshape(ROWS, COLS), prior_std, ar_rate,
            obs_var, iterate, residual, direction,
        )

    return jax.shard_map(
        per_device,
        mesh=mesh,
        in_specs=(
            P(("tm", "space"), None, None),
            P(("tm", "space"), None),
            P(("tm", "space")),
            P(("tm", "space")),
            P(None, ("tm", "space")),
            P(None, "tm", "space"),
            P("tm", "space"),
            P(None, ("tm", "space")),
            P(None, ("tm", "space")),
            P(None, ("tm", "space")),
        ),
        out_specs=(P(None, ("tm", "space")), P(None, ("tm", "space")), P(None, ("tm", "space"))),
        check_vma=False,
    )
```

time: 446 us -> 90.2 us (0.20)
  blocking collectives: 148 us -> 0 us
  waiting for transfers between devices: 104 us -> 0 us
  Pallas kernels: 0 us -> 78.4 us
  starting transfers between devices: 63 us -> 0 us
  local copies, waits for them, and re-layouts: 66.2 us -> 10.7 us
  other arithmetic: 31.5 us -> 0 us
  between operations: 15.6 us -> 0.65 us
  matrix products: 13.8 us -> 0 us
    psum x2 -> x0, blocking collectives: 148 us -> none  [the longest x1 75 us: per_device(): lax.psum((jnp.sum(begin_res * begin_res, axis=1), jnp.sum(begin_dir * ima...]
    all_gather x1 -> x0, waiting for transfers between devices: 95.3 us -> none  [per_device(): gathered = lax.all_gather(flux_half, 'space', axis=2, tiled=True)]
    pallas_call x0 -> x1, Pallas kernels: none -> 78.4 us  [per_device(): pl.pallas_call(functools.partial(kernel, n_tm, n_sp, n_x), out_shape=(vec...]
    ppermute x14 -> x0, starting transfers between devices: 41.9 us -> none  [from_behind(): return lax.ppermute(x, axis, pairs)]
    all_to_all x2 -> x0, starting transfers between devices: 21.1 us -> none  [the longest x1 11.9 us: per_device(): lax.all_to_all(desired_rows.reshape(tile_count, position_count), 'space',...]
    transpose x3 -> x0, local copies, waits for them, and re-layouts: 19.6 us -> none  [the longest x2 19.6 us: per_device(): jnp.transpose(gathered.reshape(right_count, tsteps, tile_count * nsubs, b...]
    slice x59 -> x0, local copies, waits for them, and re-layouts: 15.5 us -> none  [the longest x28 9.76 us: per_device(): lax.associative_scan(combine, (rate_rows, by_time), axis=0)]
    dot_general x5 -> x0, matrix products: 13.8 us -> none  [the longest x1 5.7 us: per_device(): jnp.dot(chooser, flux_table, preferred_element_type=jnp.float32)]
  transfers between devices with their start and end apart: 17 -> 0, of which waited for: 2 -> 0; matrix products, arithmetic and copies ran while one was open for 11% -> 0% of each run, Pallas kernels for 0% -> 0%
where the time goes in v1:
time: 90.2 us; the launch traced here: 89.8 us
  Pallas kernels  78.4 us (87%)
  local copies, waits for them, and re-layouts  10.7 us (12%)
    pallas_call x1, Pallas kernels, per_device(): pl.pallas_call(functools.partial(kernel, n_tm, n_sp, n_x), out_shape=(vec...  78.4 us
    unnamed x22, local copies, waits for them, and re-layouts  10.7 us

profile of v1, /device:TPU:1, one launch (start us, length us, event | category | flops | bytes accessed | tf_op | source)
XLA Modules:
  0.0 89.8 jit_solution(4537407099401873952)
XLA Ops:
  0.6 0.7 copy.13.btile
  1.4 0.0 copy-start
  1.4 2.2 %copy-done = bf16[16,32,4096]{2,1,0:T(8,128)(2,1)S(1)} copy-done((bf16[16,32,4096]{2,1,0:T(8,128)(2,1)S(1)}, bf16[16,32,4096]{2,1,0:T(8,128)(2,1)}, u32[]{:S(2)}) %copy-start) | copy-done | bytes 4194328
  3.6 0.0 copy-start.1
  3.6 1.0 %copy-done.1 = f32[2,32,2048]{2,1,0:T(8,128)S(1)} copy-done((f32[2,32,2048]{2,1,0:T(8,128)S(1)}, f32[2,32,2048]{2,1,0:T(8,128)}, u32[]{:S(2)}) %copy-start.1) | copy-done | bytes 524312
  4.6 0.0 copy-start.2
  4.6 0.9 %copy-done.2 = f32[32,2048]{1,0:T(8,128)S(1)} copy-done((f32[32,2048]{1,0:T(8,128)S(1)}, f32[32,2048]{1,0:T(8,128)}, u32[]{:S(2)}) %copy-start.2) | copy-done | bytes 262168
  5.5 0.0 copy-start.3
  5.5 0.7 copy-done.3
  6.2 0.0 copy-start.4
  6.2 0.7 copy-done.4
  6.9 0.0 copy-start.5
  6.9 0.7 copy-done.5
  7.6 0.0 copy-start.6
  7.6 0.7 copy-done.6
  8.3 0.0 copy-start.7
  8.3 0.7 copy-done.7
  8.9 0.0 copy-start.8
  9.0 0.7 copy-done.8
  9.6 78.4 %cg_step.1 = (f32[2,512]{1,0:T(2,128)S(1)}, f32[2,512]{1,0:T(2,128)S(1)}, f32[2,512]{1,0:T(2,128)S(1)}) custom-call(s32[16,1]{1,0:T(8,128)S(1)} %copy.13.btile, s32[16]{0:T(128)S(1)} %copy-done.7, s32[16]{0:T(128)S(1)} %copy-done.8, bf16[512,4096]{1,0:T(8,128)(2,1)S(1)} %bitcast.1, f32[2,32,2048]{2,1,0:T(8,128)S(1)} %copy-done.1, f32[32,2048]{1,0:T(8,128)S(1)} %copy-done.2, ...), custom_call_target="tpu_custom_call" | custom-call | tf_op jit(solution)/shard_map/cg_step/pallas_call | solution.py:412
  88.1 0.6 copy.17
  88.6 0.6 copy.18
  89.2 0.6 copy.19
Async XLA Ops:
  1.4 2.2 %copy-start = (bf16[16,32,4096]{2,1,0:T(8,128)(2,1)S(1)}, bf16[16,32,4096]{2,1,0:T(8,128)(2,1)}, u32[]{:S(2)}) copy-start(bf16[16,32,4096]{2,1,0:T(8,128)(2,1)} %param.10) | copy-start | bytes 12582916
  3.6 1.0 %copy-start.1 = (f32[2,32,2048]{2,1,0:T(8,128)S(1)}, f32[2,32,2048]{2,1,0:T(8,128)}, u32[]{:S(2)}) copy-start(f32[2,32,2048]{2,1,0:T(8,128)} %prior_hbm.1) | copy-start | bytes 1572868
  4.6 0.9 %copy-start.2 = (f32[32,2048]{1,0:T(8,128)S(1)}, f32[32,2048]{1,0:T(8,128)}, u32[]{:S(2)}) copy-start(f32[32,2048]{1,0:T(8,128)} %ar_hbm.1) | copy-start | bytes 786436
  5.5 0.7 copy-start.3
  6.2 0.7 copy-start.4
  6.9 0.7 copy-start.5
  7.6 0.7 copy-start.6
  8.3 0.7 copy-start.7
  8.9 0.7 copy-start.8

commit v2 on v1

--- a/solution.py
+++ b/solution.py
@@ -19,9 +19,10 @@
 
 def kernel(
     n_tm, n_sp, n_x,
-    btile, bsub, brows, fp_hbm, prior_hbm, ar_hbm, obs, iterate, residual, direction,
-    out_iter, out_res, out_dir,
-    fp, prior, rate, cbuf, prod, dep1a, dep1b, rcv1a, rcv1b, dep2a, dep2b, rcv2a, rcv2b,
+    btile_hbm, bsub_hbm, brows_hbm, fp_hbm, prior_hbm, ar_hbm, obs_hbm, iter_hbm, res_hbm, dir_hbm,
+    out_iter, out_res, out_dir, out_image, out_step, out_ratio,
+    btile, bsub, brows, obs, iterate, residual, direction,
+    fp, wide_fp, accum, prior, rate, cbuf, prod, dep1a, dep1b, rcv1a, rcv1b, dep2a, dep2b, rcv2a, rcv2b,
     meta_out, meta_in, meta_smem, first_of, second_of, onehot, back,
     coef, ends, ends_in_a, ends_in_b, rates_own, rates_in, local, carry, fluxa, fluxb, fbuf,
     red_own, red_tm, red_sum, red_sp,
@@ -33,7 +34,9 @@
     n_z = n_sp // n_x
 
     def peer(k):
-        return lax.rem(zpos + k // n_x, n_z) * n_x + lax.rem(xpos + k % n_x, n_x)
+        i = k // n_x
+        away = n_z // 2 + (i + 1) // 2 * (1 - 2 * (i % 2))
+        return lax.rem(zpos + away, n_z) * n_x + lax.rem(xpos + n_x - 1 - k % n_x, n_x)
 
     def tpeer(k):
         return lax.rem(mt + k, n_tm)
@@ -45,7 +48,20 @@
         loads.append(pltpu.make_async_copy(fp_hbm.at[:, part], fp.at[:, part], load_sem.at[c]))
     load_rate = pltpu.make_async_copy(ar_hbm, rate, load_sem.at[CHUNKS])
     load_prior = pltpu.make_async_copy(prior_hbm, prior, load_sem.at[CHUNKS + 1])
+    small = [
+        pltpu.make_async_copy(src, dst, load_sem.at[CHUNKS + 2 + i])
+        for i, (src, dst) in enumerate(
+            (
+                (btile_hbm, btile), (bsub_hbm, bsub), (brows_hbm, brows), (dir_hbm, direction),
+                (res_hbm, residual), (iter_hbm, iterate), (obs_hbm, obs),
+            )
+        )
+    ]
+    for copy in small[:4]:
+        copy.start()
     for copy in loads:
+        copy.start()
+    for copy in small[4:]:
         copy.start()
     load_rate.start()
     load_prior.start()
@@ -60,8 +76,11 @@
         pl.semaphore_signal(barrier, inc=1, device_id={"tm": tpeer(k)}, device_id_type=MESH)
         return 0
 
-    lax.fori_loop(1, n_sp, greet_space, 0)
+    lax.fori_loop(0, n_sp - 1, greet_space, 0)
     lax.fori_loop(1, n_tm, greet_tm, 0)
+
+    for copy in small:
+        copy.wait()
 
     lane = lax.broadcasted_iota(jnp.int32, (1, ROWS), 1)
     block_of = lane // OB
@@ -72,7 +91,7 @@
     begin_dir = direction[...] * valid
     begin_res = residual[...] * valid
 
-    tiles = [btile[b, 0] for b in range(NB)]
+    tiles = [btile[b] for b in range(NB)]
     place = []
     for b in range(NB):
         count = jnp.int32(0)
@@ -88,6 +107,18 @@
         wanted = jnp.where((row_j == tiles[b]) & (place_j == place[b]), bsub[b], wanted)
     meta_out[...] = (wanted * HALF + lane_j % HALF).reshape(n_sp, 1, BC)
 
+    def find(j, _):
+        first, second = jnp.int32(0), jnp.int32(0)
+        for b in range(NB - 1, -1, -1):
+            hit = btile[b] == j
+            second = jnp.where(hit, first, second)
+            first = jnp.where(hit, b, first)
+        first_of[j] = first
+        second_of[j] = second
+        return 0
+
+    lax.fori_loop(0, n_sp, find, 0)
+
     rowb = lax.broadcasted_iota(jnp.int32, (NB, ROWS), 0)
     spread = jnp.concatenate(
         [jnp.where(rowb == block_of, begin_dir[r : r + 1, :], 0.0) for r in range(2)], axis=0
@@ -134,19 +165,12 @@
         space_copy(meta_out, meta_in, peer(k), me, 0).start()
         return 0
 
-    lax.fori_loop(1, n_sp, send_meta, 0)
+    lax.fori_loop(0, n_sp - 1, send_meta, 0)
     meta_in[me] = meta_out[me]
 
     def fill_first(j):
-        first, second = jnp.int32(0), jnp.int32(0)
-        for b in range(NB - 1, -1, -1):
-            hit = btile[b, 0] == j
-            second = jnp.where(hit, first, second)
-            first = jnp.where(hit, b, first)
-        first_of[j] = first
-        second_of[j] = second
-        dep1a[j, 0] = prod[first]
-        dep1a[j, 1] = prod[second]
+        dep1a[j, 0] = prod[first_of[j]]
+        dep1a[j, 1] = prod[second_of[j]]
 
     def fill_second(j):
         dep1b[j, 0] = prod[first_of[j] + NB]
@@ -164,10 +188,10 @@
         space_copy(dep1b, rcv1b, j, me, 2).start()
         return 0
 
-    lax.fori_loop(1, n_sp, send_first, 0)
+    lax.fori_loop(0, n_sp - 1, send_first, 0)
     fill_first(me)
     rcv1a[me] = dep1a[me]
-    lax.fori_loop(1, n_sp, send_second, 0)
+    lax.fori_loop(0, n_sp - 1, send_second, 0)
     fill_second(me)
     rcv1b[me] = dep1b[me]
 
@@ -223,6 +247,13 @@
     rates_in[mt] = rates_own[...]
     load_prior.wait()
 
+    def widen(t, _):
+        at = pl.ds(pl.multiple_of(t * BC, BC), BC)
+        wide_fp[:, at] = fp[:, at].astype(F32)
+        return 0
+
+    lax.fori_loop(0, TB, widen, 0)
+
     all_arrived(meta_in, n_sp - 1, 0)
     to_smem = pltpu.make_async_copy(meta_in, meta_smem, smem_sem.at[0])
     to_smem.start()
@@ -270,7 +301,7 @@
             ends[r, 1, pl.ds(s, 1), :] = bwd[0][0:1, :]
             return 0
 
-        lax.fori_loop(0, SUB, recursions, 0)
+        lax.fori_loop(0, SUB, recursions, 0, unroll=2)
 
         def send_ends(k, _):
             who = tpeer(k)
@@ -299,7 +330,7 @@
             flux[s] = (prior[r, :, cols] * total).astype(BF16)
             return 0
 
-        lax.fori_loop(0, SUB, finish, 0)
+        lax.fori_loop(0, SUB, finish, 0, unroll=2)
 
         def fill(j):
             for p in range(CAP):
@@ -311,7 +342,7 @@
             space_copy(dep2, rcv2a if r == 0 else rcv2b, j, me, s_out).start()
             return 0
 
-        lax.fori_loop(1, n_sp, send_flux, 0)
+        lax.fori_loop(0, n_sp - 1, send_flux, 0)
         fill(me)
         (rcv2a if r == 0 else rcv2b)[me] = dep2[me]
 
@@ -324,17 +355,24 @@
         for b in range(NB):
             fbuf[b * TB : (b + 1) * TB, :] = rcv[tiles[b], place[b]].astype(F32)
 
-        def project(i, total):
-            col = pl.multiple_of(i * 2 * BC, 2 * BC)
-            left = jnp.concatenate(
-                [fbuf[pl.ds(2 * i, NB, stride=TB), :], fbuf[pl.ds(2 * i + 1, NB, stride=TB), :]], axis=1
-            ).astype(BF16)
-            return total + lax.dot_general(
-                left, fp[:, pl.ds(col, 2 * BC)], (((1,), (1,)), ((), ())), preferred_element_type=F32
+        def project(b, _):
+            own = pl.ds(pl.multiple_of(b * OB, OB), OB)
+            total = jnp.zeros((OB, BC), F32)
+            for t in range(TB):
+                total = total + wide_fp[own, t * BC : (t + 1) * BC] * fbuf[pl.ds(b * TB + t, 1), :]
+            accum[own, :] = total
+            return 0
+
+        lax.fori_loop(0, NB, project, 0, unroll=2)
+        images.append(
+            jnp.concatenate(
+                [
+                    jnp.sum(accum[i * BC : (i + 1) * BC, :].T, axis=0, keepdims=True)
+                    for i in range(ROWS // BC)
+                ],
+                axis=1,
             )
-
-        total = lax.fori_loop(0, TB // 2, project, jnp.zeros((NB, ROWS), F32))
-        images.append(jnp.sum(jnp.where(rowb == block_of, total, 0.0), axis=0, keepdims=True))
+        )
     image = jnp.concatenate(images, axis=0) * valid + obs[...] * begin_dir
 
     def partial(value):
@@ -352,6 +390,13 @@
         ],
         axis=0,
     )
+    lane8 = lax.broadcasted_iota(jnp.int32, (8, BC), 1)
+    row8 = lax.broadcasted_iota(jnp.int32, (8, BC), 0)
+
+    def as_row(column):
+        return jnp.sum(jnp.where(lane8 == row8, column, 0.0), axis=0, keepdims=True)
+
+    mine = as_row(jnp.sum(mine, axis=1, keepdims=True))
     red_own[...] = mine
     red_tm[mt] = mine
 
@@ -368,23 +413,26 @@
     red_sp[me] = part
 
     def send_sp_sum(k, _):
-        j = peer(k)
         pltpu.make_async_remote_copy(
             src_ref=red_sum, dst_ref=red_sp.at[me], send_sem=send_sem.at[9], recv_sem=recv_sem.at[9],
-            device_id={"space": j}, device_id_type=MESH,
+            device_id={"space": peer(k)}, device_id_type=MESH,
         ).start()
         return 0
 
-    lax.fori_loop(1, n_sp, send_sp_sum, 0)
+    lax.fori_loop(0, n_sp - 1, send_sp_sum, 0)
     all_arrived(red_sp, n_sp - 1, 9)
-    whole = jnp.sum(jnp.sum(red_sp[...], axis=0), axis=1, keepdims=True)
+    whole = jnp.broadcast_to(jnp.sum(red_sp[...], axis=0), (8, BC))
+    whole = jnp.sum(jnp.where(lane8 == row8, whole, 0.0), axis=1, keepdims=True)
     res_norm, curvature, cross, square = (whole[2 * i : 2 * i + 2, :] for i in range(4))
     step = res_norm / curvature
     next_norm = res_norm - 2.0 * step * cross + step * step * square
-    new_res = begin_res - step * image
-    out_iter[...] = iterate[...] * valid + step * begin_dir
-    out_res[...] = new_res
-    out_dir[...] = new_res + (next_norm / res_norm) * begin_dir
+    wide = begin_dir.shape
+    out_iter[...] = iterate[...] * valid
+    out_res[...] = begin_res
+    out_dir[...] = begin_dir
+    out_image[...] = image
+    out_step[...] = jnp.broadcast_to(step, wide)
+    out_ratio[...] = jnp.broadcast_to(next_norm / res_norm, wide)
 
     all_left(meta_out, n_sp - 1, 0)
     all_left(dep1a, n_sp - 1, 1)
@@ -404,18 +452,23 @@
 
     def per_device(footprint, block_tile, block_sub, block_rows, obs_var, prior_std, ar_rate, iterate, residual, direction):
         vmem = pl.BlockSpec(memory_space=pltpu.VMEM)
-        smem = pl.BlockSpec(memory_space=pltpu.SMEM)
         hbm = pl.BlockSpec(memory_space=pl.ANY)
         slots = pltpu.VMEM((n_sp, CAP, TB, BC), BF16)
         state = pltpu.VMEM((n_tm, SUB, BC), F32)
         vector = jax.ShapeDtypeStruct(iterate.shape, F32)
-        return pl.pallas_call(
+        begin_iter, begin_res, begin_dir, image, step, ratio = pl.pallas_call(
             functools.partial(kernel, n_tm, n_sp, n_x),
-            out_shape=(vector, vector, vector),
-            in_specs=[smem, smem, smem, hbm, hbm, hbm, vmem, vmem, vmem, vmem],
-            out_specs=(vmem, vmem, vmem),
+            out_shape=(vector,) * 6,
+            in_specs=[hbm] * 10,
+            out_specs=(vmem,) * 6,
             scratch_shapes=[
+                pltpu.SMEM(block_sub.shape, jnp.int32),
+                pltpu.SMEM(block_sub.shape, jnp.int32),
+                pltpu.SMEM(block_rows.shape, jnp.int32),
+                *[pltpu.VMEM(iterate.shape, F32)] * 4,
                 pltpu.VMEM((ROWS, COLS), BF16),
+                pltpu.VMEM((ROWS, COLS), F32),
+                pltpu.VMEM((ROWS, BC), F32),
                 pltpu.VMEM(prior_std.shape, F32),
                 pltpu.VMEM(ar_rate.shape, F32),
                 pltpu.VMEM((2 * NB * TB, BC), F32),
@@ -438,23 +491,25 @@
                 pltpu.VMEM((SUB, TB, BC), BF16),
                 pltpu.VMEM((SUB, TB, BC), BF16),
                 pltpu.VMEM((NB * TB, BC), F32),
-                pltpu.VMEM((8, BC), F32),
-                pltpu.VMEM((n_tm, 8, BC), F32),
-                pltpu.VMEM((8, BC), F32),
-                pltpu.VMEM((n_sp, 8, BC), F32),
-                pltpu.SemaphoreType.DMA((CHUNKS + 2,)),
+                pltpu.VMEM((1, BC), F32),
+                pltpu.VMEM((n_tm, 1, BC), F32),
+                pltpu.VMEM((1, BC), F32),
+                pltpu.VMEM((n_sp, 1, BC), F32),
+                pltpu.SemaphoreType.DMA((CHUNKS + 9,)),
                 pltpu.SemaphoreType.DMA((10,)),
                 pltpu.SemaphoreType.DMA((10,)),
                 pltpu.SemaphoreType.DMA((1,)),
             ],
             compiler_params=pltpu.CompilerParams(
-                collective_id=0, has_side_effects=True, vmem_limit_bytes=40 << 20
+                collective_id=0, has_side_effects=True, vmem_limit_bytes=60 << 20
             ),
             name="cg_step",
         )(
-            block_tile, block_sub, block_rows, footprint.reshape(ROWS, COLS), prior_std, ar_rate,
+            block_tile.reshape(NB), block_sub, block_rows, footprint.reshape(ROWS, COLS), prior_std, ar_rate,
             obs_var, iterate, residual, direction,
         )
+        new_res = begin_res - step * image
+        return begin_iter + step * begin_dir, new_res, new_res + ratio * begin_dir
 
     return jax.shard_map(
         per_device,

time: 90.2 us -> 74.4 us (0.82)
  local copies, waits for them, and re-layouts: 10.7 us -> 0 us
  Pallas kernels: 78.4 us -> 72.3 us
  other arithmetic: 0 us -> 1.31 us
    unnamed x22 -> x0, local copies, waits for them, and re-layouts: 10.7 us -> none
    pallas_call x1, Pallas kernels: 78.4 us -> 72.3 us  [per_device(): pl.pallas_call(functools.partial(kernel, n_tm, n_sp, n_x), out_shape=(vec...]
    add x0 -> x1, other arithmetic: none -> 1.31 us  [per_device(): return (begin_iter + step * begin_dir, new_res, new_res + ratio * begin_dir)]
where the time goes in v2:
time: 74.4 us; the launch traced here: 74.3 us
  Pallas kernels  72.3 us (97%)
  other arithmetic  1.31 us (2%)
    pallas_call x1, Pallas kernels, per_device(): pl.pallas_call(functools.partial(kernel, n_tm, n_sp, n_x), out_shape=(vec...  72.3 us

profile of v2, /device:TPU:1, one launch (start us, length us, event | category | flops | bytes accessed | tf_op | source)
XLA Modules:
  0.0 74.3 jit_solution(787311553573659264)
XLA Ops:
  0.6 72.3 %cg_step.1 = (f32[2,512]{1,0:T(2,128)}, f32[2,512]{1,0:T(2,128)}, f32[2,512]{1,0:T(2,128)}, f32[2,512]{1,0:T(2,128)}, f32[2,512]{1,0:T(2,128)}, /*index=5*/f32[2,512]{1,0:T(2,128)}) custom-call(s32[16]{0:T(128)} %bitcast.3, s32[16]{0:T(128)} %bsub_hbm.1, s32[16]{0:T(128)} %brows_hbm.1, bf16[512,4096]{1,0:T(8,128)(2,1)} %bitcast.2, f32[2,32,2048]{2,1,0:T(8,128)} %prior_hbm.1, ...), custom_call_target="tpu_custom_call" | custom-call | tf_op jit(solution)/shard_map/cg_step/pallas_call | solution.py:459
  72.9 1.3 %multiply_add_fusion = (f32[2,512]{1,0:T(2,128)}, f32[2,512]{1,0:T(2,128)}, f32[2,512]{1,0:T(2,128)}) fusion(f32[2,512]{1,0:T(2,128)} %get-tuple-element.14, f32[2,512]{1,0:T(2,128)} %get-tuple-element.11, f32[2,512]{1,0:T(2,128)} %get-tuple-element.12, f32[2,512]{1,0:T(2,128)} %get-tuple-element.10, f32[2,512]{1,0:T(2,128)} %get-tuple-element.13, ...), kind=kLoop, calls=%fused_computation | loop fusion | flops 6144 | bytes 36864 | tf_op jit(solution)/shard_map/add | solution.py:512

commit v3 on v2

--- a/solution.py
+++ b/solution.py
@@ -61,25 +61,25 @@
         copy.start()
     for copy in loads:
         copy.start()
+
+    barrier = pltpu.get_barrier_semaphore()
+
+    def greet_space(k, _):
+        pl.semaphore_signal(barrier, inc=1, device_id={"space": peer(k)}, device_id_type=MESH)
+        return 0
+
+    def greet_tm(k, _):
+        pl.semaphore_signal(barrier, inc=1, device_id={"tm": tpeer(k)}, device_id_type=MESH)
+        return 0
+
+    lax.fori_loop(0, n_sp - 1, greet_space, 0)
+    lax.fori_loop(1, n_tm, greet_tm, 0)
     for copy in small[4:]:
         copy.start()
     load_rate.start()
     load_prior.start()
 
-    barrier = pltpu.get_barrier_semaphore()
-
-    def greet_space(k, _):
-        pl.semaphore_signal(barrier, inc=1, device_id={"space": peer(k)}, device_id_type=MESH)
-        return 0
-
-    def greet_tm(k, _):
-        pl.semaphore_signal(barrier, inc=1, device_id={"tm": tpeer(k)}, device_id_type=MESH)
-        return 0
-
-    lax.fori_loop(0, n_sp - 1, greet_space, 0)
-    lax.fori_loop(1, n_tm, greet_tm, 0)
-
-    for copy in small:
+    for copy in small[:4]:
         copy.wait()
 
     lane = lax.broadcasted_iota(jnp.int32, (1, ROWS), 1)
@@ -89,7 +89,6 @@
         limit = jnp.where(block_of == b, brows[b], limit)
     valid = jnp.where(lane % OB < limit, 1.0, 0.0).astype(F32)
     begin_dir = direction[...] * valid
-    begin_res = residual[...] * valid
 
     tiles = [btile[b] for b in range(NB)]
     place = []
@@ -126,15 +125,10 @@
     for c in range(CHUNKS):
         loads[c].wait()
 
-        def product(i, _):
-            col = pl.multiple_of(c * width + i * 2 * BC, 2 * BC)
-            got = jnp.dot(spread, fp[:, pl.ds(col, 2 * BC)], preferred_element_type=F32)
-            t = c * (width // BC) + 2 * i
-            cbuf[pl.ds(t, 2 * NB, stride=TB), :] = got[:, :BC]
-            cbuf[pl.ds(t + 1, 2 * NB, stride=TB), :] = got[:, BC:]
-            return 0
-
-        lax.fori_loop(0, width // (2 * BC), product, 0)
+        got = jnp.dot(spread, fp[:, c * width : (c + 1) * width], preferred_element_type=F32)
+        for i in range(width // BC):
+            t = c * (width // BC) + i
+            cbuf[pl.ds(t, 2 * NB, stride=TB), :] = got[:, i * BC : (i + 1) * BC]
 
     for i in range(2 * NB):
         prod[i] = cbuf[i * TB : (i + 1) * TB, :].astype(BF16)
@@ -165,8 +159,6 @@
         space_copy(meta_out, meta_in, peer(k), me, 0).start()
         return 0
 
-    lax.fori_loop(0, n_sp - 1, send_meta, 0)
-    meta_in[me] = meta_out[me]
 
     def fill_first(j):
         dep1a[j, 0] = prod[first_of[j]]
@@ -188,7 +180,10 @@
         space_copy(dep1b, rcv1b, j, me, 2).start()
         return 0
 
-    lax.fori_loop(0, n_sp - 1, send_first, 0)
+    lax.fori_loop(0, 8, send_first, 0)
+    lax.fori_loop(0, n_sp - 1, send_meta, 0)
+    meta_in[me] = meta_out[me]
+    lax.fori_loop(8, n_sp - 1, send_first, 0)
     fill_first(me)
     rcv1a[me] = dep1a[me]
     lax.fori_loop(0, n_sp - 1, send_second, 0)
@@ -348,6 +343,10 @@
 
     owner(0, rcv1a, fluxa, dep2a, ends_in_a, 1, 4, 6)
     owner(1, rcv1b, fluxb, dep2b, ends_in_b, 2, 5, 7)
+
+    for copy in small[4:]:
+        copy.wait()
+    begin_res = residual[...] * valid
 
     images = []
     for r, (rcv, s_out) in enumerate(((rcv2a, 6), (rcv2b, 7))):

time: 74.4 us -> 72.8 us (0.978)
  Pallas kernels: 72.3 us -> 70.7 us
    pallas_call x1, Pallas kernels: 72.3 us -> 70.7 us  [per_device(): pl.pallas_call(functools.partial(kernel, n_tm, n_sp, n_x), out_shape=(vec...]
where the time goes in v3:
time: 72.8 us; the launch traced here: 72.7 us
  Pallas kernels  70.7 us (97%)
  other arithmetic  1.31 us (2%)
    pallas_call x1, Pallas kernels, per_device(): pl.pallas_call(functools.partial(kernel, n_tm, n_sp, n_x), out_shape=(vec...  70.7 us

profile of v3, /device:TPU:1, one launch (start us, length us, event | category | flops | bytes accessed | tf_op | source)
XLA Modules:
  0.0 72.7 jit_solution(17153968747214857828)
XLA Ops:
  0.6 70.7 %cg_step.1 = (f32[2,512]{1,0:T(2,128)}, f32[2,512]{1,0:T(2,128)}, f32[2,512]{1,0:T(2,128)}, f32[2,512]{1,0:T(2,128)}, f32[2,512]{1,0:T(2,128)}, /*index=5*/f32[2,512]{1,0:T(2,128)}) custom-call(s32[16]{0:T(128)} %bitcast.3, s32[16]{0:T(128)} %bsub_hbm.1, s32[16]{0:T(128)} %brows_hbm.1, bf16[512,4096]{1,0:T(8,128)(2,1)} %bitcast.2, f32[2,32,2048]{2,1,0:T(8,128)} %prior_hbm.1, ...), custom_call_target="tpu_custom_call" | custom-call | tf_op jit(solution)/shard_map/cg_step/pallas_call | solution.py:458
  71.4 1.3 %multiply_add_fusion = (f32[2,512]{1,0:T(2,128)}, f32[2,512]{1,0:T(2,128)}, f32[2,512]{1,0:T(2,128)}) fusion(f32[2,512]{1,0:T(2,128)} %get-tuple-element.14, f32[2,512]{1,0:T(2,128)} %get-tuple-element.11, f32[2,512]{1,0:T(2,128)} %get-tuple-element.12, f32[2,512]{1,0:T(2,128)} %get-tuple-element.10, f32[2,512]{1,0:T(2,128)} %get-tuple-element.13, ...), kind=kLoop, calls=%fused_computation | loop fusion | flops 6144 | bytes 36864 | tf_op jit(solution)/shard_map/add | solution.py:511

commit v4 on v3

--- a/solution.py
+++ b/solution.py
@@ -34,9 +34,9 @@
     n_z = n_sp // n_x
 
     def peer(k):
-        i = k // n_x
+        i = k % n_z
         away = n_z // 2 + (i + 1) // 2 * (1 - 2 * (i % 2))
-        return lax.rem(zpos + away, n_z) * n_x + lax.rem(xpos + n_x - 1 - k % n_x, n_x)
+        return lax.rem(zpos + away, n_z) * n_x + lax.rem(xpos + n_x - 1 - k // n_z, n_x)
 
     def tpeer(k):
         return lax.rem(mt + k, n_tm)
@@ -419,6 +419,16 @@
         return 0
 
     lax.fori_loop(0, n_sp - 1, send_sp_sum, 0)
+    all_left(meta_out, n_sp - 1, 0)
+    all_left(dep1a, n_sp - 1, 1)
+    all_left(dep1b, n_sp - 1, 2)
+    all_left(rates_in, n_tm - 1, 3)
+    all_left(ends_in_a, n_tm - 1, 4)
+    all_left(ends_in_b, n_tm - 1, 5)
+    all_left(dep2a, n_sp - 1, 6)
+    all_left(dep2b, n_sp - 1, 7)
+    all_left(red_tm, n_tm - 1, 8)
+    all_left(red_sp, n_sp - 1, 9)
     all_arrived(red_sp, n_sp - 1, 9)
     whole = jnp.broadcast_to(jnp.sum(red_sp[...], axis=0), (8, BC))
     whole = jnp.sum(jnp.where(lane8 == row8, whole, 0.0), axis=1, keepdims=True)
@@ -432,17 +442,6 @@
     out_image[...] = image
     out_step[...] = jnp.broadcast_to(step, wide)
     out_ratio[...] = jnp.broadcast_to(next_norm / res_norm, wide)
-
-    all_left(meta_out, n_sp - 1, 0)
-    all_left(dep1a, n_sp - 1, 1)
-    all_left(dep1b, n_sp - 1, 2)
-    all_left(rates_in, n_tm - 1, 3)
-    all_left(ends_in_a, n_tm - 1, 4)
-    all_left(ends_in_b, n_tm - 1, 5)
-    all_left(dep2a, n_sp - 1, 6)
-    all_left(dep2b, n_sp - 1, 7)
-    all_left(red_tm, n_tm - 1, 8)
-    all_left(red_sp, n_sp - 1, 9)
 
 
 def solution(mesh):

time: 72.8 us -> 71.8 us (0.986)
  Pallas kernels: 70.7 us -> 69.7 us
    pallas_call x1, Pallas kernels: 70.7 us -> 69.7 us  [per_device(): pl.pallas_call(functools.partial(kernel, n_tm, n_sp, n_x), out_shape=(vec...]
where the time goes in v4:
time: 71.8 us; the launch traced here: 71.7 us
  Pallas kernels  69.7 us (97%)
  other arithmetic  1.31 us (2%)
    pallas_call x1, Pallas kernels, per_device(): pl.pallas_call(functools.partial(kernel, n_tm, n_sp, n_x), out_shape=(vec...  69.7 us

profile of v4, /device:TPU:1, one launch (start us, length us, event | category | flops | bytes accessed | tf_op | source)
XLA Modules:
  0.0 71.7 jit_solution(4228702060436302799)
XLA Ops:
  0.6 69.7 %cg_step.1 = (f32[2,512]{1,0:T(2,128)}, f32[2,512]{1,0:T(2,128)}, f32[2,512]{1,0:T(2,128)}, f32[2,512]{1,0:T(2,128)}, f32[2,512]{1,0:T(2,128)}, /*index=5*/f32[2,512]{1,0:T(2,128)}) custom-call(s32[16]{0:T(128)} %bitcast.3, s32[16]{0:T(128)} %bsub_hbm.1, s32[16]{0:T(128)} %brows_hbm.1, bf16[512,4096]{1,0:T(8,128)(2,1)} %bitcast.2, f32[2,32,2048]{2,1,0:T(8,128)} %prior_hbm.1, ...), custom_call_target="tpu_custom_call" | custom-call | tf_op jit(solution)/shard_map/cg_step/pallas_call | solution.py:457
  70.4 1.3 %multiply_add_fusion = (f32[2,512]{1,0:T(2,128)}, f32[2,512]{1,0:T(2,128)}, f32[2,512]{1,0:T(2,128)}) fusion(f32[2,512]{1,0:T(2,128)} %get-tuple-element.14, f32[2,512]{1,0:T(2,128)} %get-tuple-element.11, f32[2,512]{1,0:T(2,128)} %get-tuple-element.12, f32[2,512]{1,0:T(2,128)} %get-tuple-element.10, f32[2,512]{1,0:T(2,128)} %get-tuple-element.13, ...), kind=kLoop, calls=%fused_computation | loop fusion | flops 6144 | bytes 36864 | tf_op jit(solution)/shard_map/add | solution.py:510
